TPU v7x, 128 devices: a whole 4x4x4 slice. The times are simulated.
128 devices in a mesh: tx: 16 (over y, z), ty: 8 (over x, core).
Axes of the slice: x: 4, y: 4, z: 4, core: 2. Of those that a mesh axis runs over, the one named last changes fastest.
Arguments:
- increments: bfloat16 [1536, 1536, 128], P('ty', 'tx'), may hold values from -6 to 6
- lengths: float32 [4, 3], replicated, may hold values from 2 to 768
- lat_class: int32 [1536], replicated, may hold values from 0 to 3
- slab_owner: int32 [128], replicated, may hold values from 0 to 127, as said below
- level_sigma: float32 [128], replicated, may hold values from 0.5 to 4
Outputs:
- smoothed: bfloat16 [1536, 1536, 128], P('ty', 'tx')
- peak_table: float32 [128, 2], P(('tx', 'ty'))
Inputs may be any that keep to these rules, and one draw needn't show every extreme that they name: `slab_owner`: no device owns more than 2 slabs; some devices own exactly 2, some none.
All inputs are finite; a program needn't handle non-finite values.
Results may differ from a plain program's by a relative error of at most 0.006.
Values may be sent and summed in bfloat16 or wider, within the bound.
No kernel may reach another device: no remote copies, remote signals or barrier semaphores. Data moves between devices by JAX's collectives and lax.ppermute only.
A program may use at most 192 MiB of HBM per device.

v0:
```python
import functools

import jax
import jax.numpy as jnp
from jax import lax
from jax.experimental import pallas as pl
from jax.experimental.pallas import tpu as pltpu
from jax.sharding import PartitionSpec as P

NCLASS = 4
MOST = 2
SCALE_WEIGHTS = (0.5, 0.35, 0.25)
LOG, RATE, FWD, BWD, INV = 0, 3, 6, 9, 12
GROUP = 8
BLOCK = 16
LONG = 48
TURNS = 6
CHUNK = 48
F32, BF16 = jnp.float32, jnp.bfloat16


def iota(shape, axis):
    return lax.broadcasted_iota(jnp.int32, shape, axis)


def class_rows(lengths_ref, lanes):
    rows = []
    for c in range(NCLASS):
        log = [-1.0 / jnp.full((1, lanes), lengths_ref[c, k], F32) for k in range(3)]
        rate = [jnp.exp(log[k]) for k in range(3)]
        forward = [SCALE_WEIGHTS[k] * jnp.sqrt(1.0 - rate[k] * rate[k]) for k in range(3)]
        backward = [SCALE_WEIGHTS[k] * (1.0 - rate[k]) for k in range(3)]
        inverse = [1.0 / (1.0 - rate[k] * rate[q]) for q in range(3) for k in range(3)]
        rows.append(log + rate + forward + backward + inverse)
    return rows


class Pieces:
    def __init__(self, source, target, done, rows):
        self.source, self.target, self.done, self.rows = source, target, done, rows
        self.count = source.shape[0] // rows

    def copy(self, piece):
        rows = pl.ds(pl.multiple_of(piece * self.rows, self.rows), self.rows)
        return pltpu.make_async_copy(self.source.at[rows], self.target.at[rows], self.done.at[piece])

    def start(self, order=None):
        for piece in range(self.count) if order is None else order:
            self.copy(piece).start()

    def wait(self):
        for piece in range(self.count):
            self.copy(piece).wait()


def start_all(sources, targets, done):
    copies = [
        pltpu.make_async_copy(source, target, done.at[i])
        for i, (source, target) in enumerate(zip(sources, targets))
    ]
    for copy in copies:
        copy.start()

    def wait():
        for copy in copies:
            copy.wait()

    return wait


def class_reader(rows, c, lanes):
    return lambda at: rows[c][at][:, :lanes]


def ends_kernel(lat_ref, lengths_ref, v_ref, e_ref, w_ref, here_ref, arrived):
    height, width, lanes = v_ref.shape
    tile = lax.axis_index("ty") * height
    pieces = Pieces(v_ref, here_ref, arrived, LONG)
    pieces.start()
    shape = (GROUP, width)
    row = iota(shape, 0)
    at = iota(shape, 1).astype(F32)
    totals = []
    for c in range(NCLASS):
        log = [-1.0 / jnp.full(shape, lengths_ref[c, k], F32) for k in range(3)]
        rate = [jnp.exp(log[k]) for k in range(3)]
        fwd = [SCALE_WEIGHTS[k] * jnp.sqrt(1.0 - rate[k] * rate[k]) for k in range(3)]
        rest = [jnp.exp(log[k] * (width - at)) for k in range(3)]
        total = jnp.zeros(shape, F32)
        for k in range(3):
            fwd_end = fwd[k] * jnp.exp(log[k] * (width - 1 - at))
            total = jnp.where(row == k, fwd_end, total)
        for q in range(3):
            back = jnp.zeros(shape, F32)
            for k in range(3):
                back += fwd[k] * (1.0 - rest[k] * rest[q]) / (1.0 - rate[k] * rate[q])
            back = back * (SCALE_WEIGHTS[q] * (1.0 - rate[q])) * jnp.exp(log[q] * at)
            total = jnp.where(row == 3 + q, back, total)
        totals.append(total)
    for c in range(NCLASS):
        for d in range(NCLASS):
            w_ref[NCLASS * c + d] = jnp.concatenate([totals[c], totals[d]], axis=0).astype(BF16)

    def run(step, _):
        pieces.copy(step).wait()
        for r in range(0, LONG, 2):
            row = step * LONG + r
            pair = NCLASS * lat_ref[tile + row] + lat_ref[tile + row + 1]
            both = jnp.concatenate([here_ref[row], here_ref[row + 1]], axis=1)
            done = jnp.dot(w_ref[pair], both, preferred_element_type=F32)
            own = jnp.concatenate([done[:GROUP, :lanes], done[GROUP:, lanes:]], axis=0)
            at = pl.multiple_of(row * GROUP, 2 * GROUP)
            e_ref[pl.ds(at, 2 * GROUP), :] = own.astype(BF16)
        return 0

    lax.fori_loop(0, pieces.count, run, 0)


def scan_kernel(width, height, lat_ref, lengths_ref, e_ref, c_ref, decay_ref, cross_ref, f_ref):
    devices, lines, lanes = e_ref.shape
    fill_scan_tables(lat_ref, lengths_ref, width, height, decay_ref, cross_ref)
    decay = decay_ref[...]
    cross = cross_ref[:, :lines]
    state = jnp.zeros((lines, lanes), F32)
    for t in range(devices):
        f_ref[t] = state
        state = decay * state + e_ref[t].astype(F32)
    kind = iota((lines, lanes), 0) % GROUP
    state = jnp.zeros((lines, lanes), F32)
    for t in range(devices - 1, -1, -1):
        ahead = f_ref[t]
        c_ref[t] = jnp.where(kind < 3, ahead, jnp.where(kind < 6, state, 0.0)).astype(BF16)
        if t > 0:
            turned = jnp.dot(cross, ahead.astype(BF16), preferred_element_type=F32)
            state = decay * state + e_ref[t].astype(F32) + turned


def fill_scan_tables(lat_ref, lengths_ref, width, height, decay_ref, cross_ref):
    lines, lanes = decay_ref.shape
    rows = lines // GROUP
    first = lax.axis_index("ty") * height + lax.axis_index("tx") * rows
    row = iota((GROUP, lanes), 0)
    lane = iota((GROUP, lanes), 1)
    decay, cross = [], []
    for c in range(NCLASS):
        logs = [-1.0 / jnp.full((GROUP, lanes), lengths_ref[c, k], F32) for k in range(3)]
        rate = [jnp.exp(logs[k]) for k in range(3)]
        far = [jnp.exp(logs[k] * width) for k in range(3)]
        hold = jnp.zeros((GROUP, lanes), F32)
        mix = jnp.zeros((GROUP, lanes), F32)
        for k in range(3):
            hold = jnp.where((row == k) | (row == 3 + k), far[k], hold)
            for q in range(3):
                value = (SCALE_WEIGHTS[q] * (1.0 - rate[q])) * rate[k] * (
                    (1.0 - far[k] * far[q]) / (1.0 - rate[k] * rate[q])
                )
                mix = jnp.where((row == 3 + q) & (lane % GROUP == k), value, mix)
        decay.append(hold)
        cross.append(mix)
    for r in range(0, rows, 2):
        mixes = []
        for at in (r, r + 1):
            c = lat_ref[first + at]
            d, m = decay[0], cross[0]
            for other in range(1, NCLASS):
                d = jnp.where(c == other, decay[other], d)
                m = jnp.where(c == other, cross[other], m)
            decay_ref[pl.ds(at * GROUP, GROUP), :] = d
            mixes.append(jnp.where(lane // GROUP == at, m, 0.0))
        cross_ref[pl.ds(r * GROUP, 2 * GROUP), :] = jnp.concatenate(mixes, axis=0).astype(BF16)


def x_table_parts(rows, c, width, depth):
    get = class_reader(rows, c, depth)
    out_at = iota((width, depth), 0).astype(F32)
    lane = iota((width, depth), 1)
    in_at = lane.astype(F32)
    far = jnp.maximum(out_at, in_at)
    later = out_at >= in_at
    gap = jnp.abs(out_at - in_at)
    near_power = [jnp.exp(get(LOG + k) * gap) for k in range(3)]
    rest_power = [jnp.exp(get(LOG + k) * jnp.maximum(width - far, 0.0)) for k in range(3)]
    own_rest = [jnp.exp(get(LOG + k) * (width - out_at)) for k in range(3)]
    inner = jnp.zeros((width, depth), F32)
    carried = [jnp.zeros((width, depth), F32) for _ in range(3)]
    for q in range(3):
        for k in range(3):
            inverse = get(INV + 3 * q + k)
            inner += (get(FWD + k) * get(BWD + q) * inverse) * (
                jnp.where(later, near_power[k], near_power[q])
                * (1.0 - rest_power[k] * rest_power[q])
            )
            carried[k] += (get(BWD + q) * inverse) * (1.0 - own_rest[k] * own_rest[q])
    inner = jnp.where(lane < width, inner, 0.0)
    for k in range(3):
        carried[k] = carried[k] * jnp.exp(get(LOG + k) * (out_at + 1.0))
    return lane, inner, carried + own_rest


EXACT = dict(precision=lax.Precision.HIGHEST, preferred_element_type=F32)


def of_class(rows, lat, at):
    lanes = lat.shape[1]
    value = jnp.broadcast_to(rows[0][at][:, :lanes], lat.shape)
    for c in range(1, NCLASS):
        value = jnp.where(lat == c, rows[c][at][:, :lanes], value)
    return value


def over_points(rows):
    height = rows.shape[1]
    long = height * GROUP
    wider = (iota((height, long), 1) // GROUP == iota((height, long), 0)).astype(BF16)
    wide = jnp.dot(rows.astype(BF16), wider, preferred_element_type=F32)
    same = iota((GROUP, long), 1) % GROUP == iota((GROUP, long), 0)
    spread = [jnp.where(same, wide[q : q + 1], 0.0) for q in range(6)]
    return wide, jnp.concatenate(spread, axis=0).astype(BF16)


def tables_kernel(
    lengths_ref, lat_ref, m_ref, x_ref, y_ref, corner_ref,
    own_ref, ends_ref, local_ref, scan_ref,
):
    _, width, depth = m_ref.shape
    lanes = y_ref.shape[2]
    devices = y_ref.shape[1]
    height = lat_ref.shape[0] * lat_ref.shape[1] // devices
    rows = class_rows(lengths_ref, 2 * lanes)
    flat = lat_ref[...].astype(F32)
    flat = jnp.concatenate([flat[i : i + 1] for i in range(lat_ref.shape[0])], axis=1)
    lat = [flat[:, u * height : (u + 1) * height] for u in range(devices)]
    lat = jnp.concatenate(lat, axis=0)
    spread = jnp.zeros((width, depth), F32)
    for c in range(NCLASS):
        lane, inner, states = x_table_parts(rows, c, width, depth)
        for parity in range(2):
            table = inner
            for k in range(6):
                table = jnp.where(lane == width + GROUP * parity + k, states[k], table)
            m_ref[2 * c + parity] = table.astype(BF16)
        for k in range(6):
            spread = jnp.where(lane == c * GROUP + k, states[k], spread)
    x_ref[...] = spread[:, : x_ref.shape[1]].astype(BF16)

    def by_class(lat, at):
        return of_class(rows, lat, at)

    row, column = iota((height, height), 0), iota((height, height), 1)
    upto = (row <= column).astype(F32)
    logs = [by_class(lat, LOG + k) for k in range(3)]
    level = jnp.dot(jnp.concatenate(logs, axis=0), upto, **EXACT)
    levels = [level[k * devices : (k + 1) * devices] for k in range(3)]
    reach = [jnp.exp(levels[k]) for k in range(3)]
    cross = []
    for q in range(3):
        gain = by_class(lat, BWD + q) * jnp.exp(levels[q] - logs[q])
        for k in range(3):
            mixed = jnp.sum(gain * reach[k], axis=1, keepdims=True)
            cross.append(jnp.broadcast_to(mixed, (devices, lanes)))
    fill_y_tables(levels, cross, y_ref)

    mine = iota(lat.shape, 0) == lax.axis_index("ty")
    own = jnp.sum(jnp.where(mine, lat, 0.0), axis=0, keepdims=True)
    own = jnp.broadcast_to(own, (GROUP, height))
    fill_block_tables(rows, own, ends_ref, local_ref, scan_ref)
    _, _, ends, _, _, _, _ = two_passes(rows, own, row >= 0)
    total, own_ref[...] = over_points(ends)
    corner_ref[...] = total


def two_passes(rows, lat, same):
    height = lat.shape[1]
    lanes = 128
    kind = iota((GROUP, height), 0)
    row, column = iota((height, height), 0), iota((height, height), 1)
    log = jnp.zeros((GROUP, height), F32)
    forward = jnp.zeros((GROUP, height), F32)
    backward = jnp.zeros((GROUP, height), F32)
    for k in range(3):
        log = jnp.where(kind == k, of_class(rows, lat, LOG + k), log)
        forward = jnp.where(kind == k, of_class(rows, lat, FWD + k), forward)
        backward = jnp.where(kind == k, of_class(rows, lat, BWD + k), backward)
    turn = (((1,), (1,)), ((), ()))
    upto = jnp.dot(log, (same & (row <= column)).astype(F32), **EXACT)
    every = jnp.dot(log, same.astype(F32), **EXACT)
    before = upto - log
    upto_down = lax.dot_general((same & (column <= row)).astype(F32), log, turn, **EXACT)
    before_down = lax.dot_general((same & (column < row)).astype(F32), log, turn, **EXACT)
    every_down = lax.dot_general(same.astype(F32), log, turn, **EXACT)
    ahead = jnp.zeros((height, height), F32)
    back = jnp.zeros((height, height), F32)
    for k in range(3):
        gap = jnp.minimum(upto_down[:, k : k + 1] - upto[k : k + 1], 0.0)
        ahead += jnp.exp(gap) * forward[k : k + 1]
        gap = jnp.minimum(before[k : k + 1] - before_down[:, k : k + 1], 0.0)
        back += jnp.exp(gap) * backward[k : k + 1]
    ahead = jnp.where(same & (row >= column), ahead, 0.0)
    back = jnp.where(same & (row <= column), back, 0.0)

    gain = backward * jnp.exp(before)
    turned = jnp.dot(gain, ahead, **EXACT)
    ends = [(forward * jnp.exp(every - upto))[:3], turned[:3], lat[:1].astype(F32), lat[:1].astype(F32)]
    from_ahead = jnp.dot(back, jnp.exp(upto_down), **EXACT)
    from_back = jnp.exp(every_down - before_down)
    lane = iota((height, lanes), 1)
    entering = jnp.zeros((height, lanes), F32)
    for k in range(3):
        entering = jnp.where(lane % 48 // GROUP == k, from_ahead[:, k : k + 1], entering)
        entering = jnp.where(lane % 48 // GROUP == 3 + k, from_back[:, k : k + 1], entering)
    rest = entering - entering.astype(BF16).astype(F32)
    entering = jnp.where(lane < 48, entering, jnp.where(lane < 96, rest, 0.0)).astype(BF16)
    return ahead, back, jnp.concatenate(ends, axis=0), entering, gain, upto, every


def fill_block_tables(rows, lat, ends_ref, local_ref, scan_ref):
    height = lat.shape[1]
    blocks, _, lanes = scan_ref.shape
    same = iota((height, height), 0) // BLOCK == iota((height, height), 1) // BLOCK
    ahead, back, ends, entering, gain, upto, every = two_passes(rows, lat, same)
    _, ends_ref[...] = over_points(ends)

    reach = jnp.exp(upto)
    steps = [jnp.exp(every)[:3]]
    for q in range(3):
        steps.append(jnp.dot(gain[q : q + 1] * reach, same.astype(F32), **EXACT)[:3])
    steps = jnp.concatenate(steps + [jnp.zeros((4, height), F32)], axis=0)
    pick = (iota((height, lanes), 0) == iota((height, lanes), 1) * BLOCK).astype(F32)
    steps = jnp.dot(steps, pick, **EXACT)
    for block in range(blocks):
        scan_ref[block] = jnp.broadcast_to(steps[:, block : block + 1], steps.shape)

    inner = jnp.dot(back, ahead, **EXACT)
    fold = (iota((height, lanes), 0) % BLOCK == iota((height, lanes), 1) // GROUP).astype(BF16)
    inner = jnp.dot(inner.astype(BF16), fold, preferred_element_type=F32).astype(BF16)
    local_ref[...] = jnp.concatenate([inner, entering], axis=1)


def each_point(rows):
    count = rows.shape[0]
    long = count * GROUP
    taller = (iota((long, count), 0) // GROUP == iota((long, count), 1)).astype(BF16)
    whole = jnp.dot(taller, rows, preferred_element_type=F32)
    same_point = iota(whole.shape, 0) % GROUP == iota(whole.shape, 1) % GROUP
    return jnp.where(same_point, whole, 0.0).astype(BF16)


def fill_y_tables(levels, cross, y_ref):
    _, devices, lanes = y_ref.shape
    mine = lax.axis_index("ty")
    row = iota((devices, lanes), 0)
    before, upto, my_before, my_upto = [], [], [], []
    for k in range(3):
        level = jnp.broadcast_to(levels[k][:, -1:], (devices, lanes))
        total = jnp.zeros((devices, lanes), F32)
        for u in range(devices - 1):
            total += jnp.where(row > u, level[u : u + 1], 0.0)
        before.append(total)
        upto.append(total + level)
        my_before.append(jnp.sum(jnp.where(row == mine, total, 0.0), axis=0, keepdims=True))
        my_upto.append(jnp.sum(jnp.where(row == mine, total + level, 0.0), axis=0, keepdims=True))
        y_ref[12 + k] = jnp.broadcast_to(jnp.exp(my_upto[k] - my_before[k]), (devices, lanes))

    def decay(gap):
        return jnp.exp(jnp.minimum(gap, 0.0))

    for q in range(3):
        y_ref[q] = jnp.where(row < mine, decay(my_before[q] - upto[q]), 0.0)
        back = [decay(before[q][u : u + 1] - upto[q]) for u in range(devices)]
        for k in range(3):
            turned = jnp.zeros((devices, lanes), F32)
            for u in range(1, devices):
                ahead = decay(before[k][u : u + 1] - my_upto[k]) * cross[3 * q + k][u : u + 1]
                turned += jnp.where(mine < u, back[u] * ahead, 0.0)
            straight = decay(before[k] - my_upto[k]) if q == k else 0.0
            y_ref[3 + 3 * q + k] = jnp.where(row > mine, straight, turned)


def block_rows(step):
    lines = BLOCK * GROUP
    return pl.ds(pl.multiple_of(step * lines, lines), lines)


def store_points(wide_ref, row, pair):
    width, lanes = pair[0].shape
    at = pl.multiple_of(row * GROUP, 2 * GROUP)
    for piece in range(width // (2 * GROUP)):
        for half in range(2):
            rows = slice((2 * piece + half) * GROUP, (2 * piece + half + 1) * GROUP)
            both = jnp.concatenate([pair[0][rows], pair[1][rows]], axis=0)
            here = slice(half * lanes, (half + 1) * lanes)
            wide_ref[piece, pl.ds(at, 2 * GROUP), here] = both.astype(BF16)


def own_ends_kernel(
    lat_ref, v_ref, m_far, weight_far,
    e_ref, sum_ref, even_ref, odd_ref, here_ref, arrived, m_ref, weight_ref, fetched,
):
    height, width, lanes = v_ref.shape
    pieces = Pieces(v_ref, here_ref, arrived, 2 * BLOCK)
    wait = start_all([m_far, weight_far], [m_ref, weight_ref], fetched)
    pieces.start()
    tile = lax.axis_index("ty") * height
    sum_ref[...] = jnp.zeros_like(sum_ref)

    def along_x(step, block_ref):
        for r in range(0, BLOCK, 2):
            pair = []
            for at in (r, r + 1):
                row = step * BLOCK + at
                table = m_ref[2 * lat_ref[tile + row]][:, :width]
                pair.append(jnp.dot(table, here_ref[row], preferred_element_type=F32))
            store_points(block_ref, r, pair)

    def along_y(step, block_ref):
        weight = weight_ref[:, block_rows(step)]
        for piece in range(sum_ref.shape[0]):
            sum_ref[piece] += jnp.dot(weight, block_ref[piece], preferred_element_type=F32)

    wait()
    in_turn(pieces, along_x, along_y, even_ref, odd_ref)
    for piece in range(sum_ref.shape[0]):
        for half in range(2):
            for q in range(6):
                here = pl.ds((2 * piece + half) * GROUP, GROUP)
                part = sum_ref[piece, pl.ds(q * GROUP, GROUP), half * lanes : (half + 1) * lanes]
                e_ref[q, here, :] = part


def corner_kernel(corner_ref, c_ref, x_ref, own_ref, y_ref, send_ref, e_ref):
    group = x_ref.shape[1]
    devices = send_ref.shape[0]
    _, width, _ = own_ref.shape
    long = corner_ref.shape[1]
    pick = iota((group, long), 0)
    chosen = (corner_ref[pl.ds(6, 1), :] == (pick // GROUP).astype(F32)) & (
        iota((group, long), 1) % GROUP == pick % GROUP
    )
    corner = [jnp.where(chosen, corner_ref[pl.ds(q, 1), :], 0.0).astype(BF16) for q in range(6)]
    corner = jnp.concatenate(corner, axis=0)
    sums = jnp.dot(corner, c_ref[...], preferred_element_type=F32).astype(BF16)
    for q in range(6):
        part = sums[q * group : (q + 1) * group]
        e_ref[q] = own_ref[q] + jnp.dot(x_ref[...], part, preferred_element_type=F32)
    for at in range(0, width, CHUNK):
        ends = [e_ref[q, pl.ds(at, CHUNK), :] for q in range(6)]
        for u in range(devices):
            for q in range(3):
                total = y_ref[q, pl.ds(u, 1), :] * ends[3 + q]
                for k in range(3):
                    total += y_ref[3 + 3 * q + k, pl.ds(u, 1), :] * ends[k]
                send_ref[u, pl.ds(q * width + at, CHUNK), :] = total.astype(BF16)


def in_turn(pieces, produce, use, even_ref, odd_ref):
    steps = 2 * pieces.count
    pieces.copy(0).wait()
    produce(0, even_ref)

    def pair(i, _):
        pieces.copy(i + 1).wait()
        produce(2 * i + 1, odd_ref)
        use(2 * i, even_ref)
        produce(2 * i + 2, even_ref)
        use(2 * i + 1, odd_ref)
        return 0

    lax.fori_loop(0, pieces.count - 1, pair, 0)
    produce(steps - 1, odd_ref)
    use(steps - 2, even_ref)
    use(steps - 1, odd_ref)


def filter_kernel(
    lat_ref, v_ref, c_far, m_far, ends_far, after_ref,
    wide_far, end_far, c_ref, m_ref, ends_ref, fetched, even_ref, odd_ref, wide_ref, end_ref,
    here_ref, arrived, sent, end_sent,
):
    del after_ref
    height, width, lanes = v_ref.shape
    pieces = Pieces(v_ref, here_ref, arrived, 2 * BLOCK)
    results = Pieces(wide_ref, wide_far, sent, 1)
    end_results = Pieces(end_ref, end_far, end_sent, 1)
    wait = start_all([c_far, m_far, ends_far], [c_ref, m_ref, ends_ref], fetched)
    pieces.start()
    tile = lax.axis_index("ty") * height

    def along_x(step, block_ref):
        for r in range(0, BLOCK, 2):
            pair = []
            at = pl.multiple_of((step * BLOCK + r) * GROUP, 2 * GROUP)
            states = c_ref[pl.ds(at, 2 * GROUP), :]
            for parity in range(2):
                row = step * BLOCK + r + parity
                right = jnp.concatenate([here_ref[row], states], axis=0)
                table = m_ref[2 * lat_ref[tile + row] + parity]
                pair.append(jnp.dot(table, right, preferred_element_type=F32))
            store_points(block_ref, r, pair)

    def ends(step, block_ref):
        weight = ends_ref[:, block_rows(step)]
        for piece in range(wide_ref.shape[1]):
            block = block_ref[piece]
            wide_ref[step, piece] = block
            done = jnp.dot(weight, block, preferred_element_type=F32)
            end_ref[step, piece] = done.astype(BF16)
        results.copy(step).start()
        end_results.copy(step).start()

    wait()
    in_turn(pieces, along_x, ends, even_ref, odd_ref)
    results.wait()
    end_results.wait()


def y_carries(y_ref, arrived_ref, f_ref):
    devices = arrived_ref.shape[0]
    lanes = arrived_ref.shape[2]
    width = arrived_ref.shape[1] // 3
    mine = lax.axis_index("ty")
    mixed = [
        [
            y_ref[3 + 3 * q + k, pl.ds(mine, 1), :] * y_ref[12 + k, pl.ds(0, 1), :]
            for k in range(3)
        ]
        for q in range(3)
    ]
    for at in range(0, width, 2 * GROUP):
        ahead = [jnp.zeros((2 * GROUP, lanes), F32) for _ in range(3)]
        back = list(ahead)
        for u in range(devices):
            for q in range(3):
                came = arrived_ref[u, pl.ds(q * width + at, 2 * GROUP), :].astype(F32)
                ahead[q] += jnp.where(u < mine, came, 0.0)
                back[q] += jnp.where(u < mine, 0.0, came)
        states = list(ahead)
        for q in range(3):
            total = back[q]
            for k in range(3):
                total += mixed[q][k] * ahead[k]
            states.append(total)
        for half in range(2):
            for k in range(6):
                part = states[k][half * GROUP : (half + 1) * GROUP]
                place = pl.ds(k * GROUP, GROUP)
                f_ref[at // (2 * GROUP), place, half * lanes : (half + 1) * lanes] = part


def scan_blocks(scan_ref, end_ref, f_ref, ahead_ref, state_ref):
    steps, count, _, _ = end_ref.shape

    def at(k):
        return pl.ds(k * GROUP, GROUP)

    def factor(step, plane):
        row = scan_ref[step, pl.ds(plane, 1), :]
        return jnp.concatenate([row, row], axis=1)

    def two(step, piece, k):
        pair = end_ref[step, piece, pl.ds(k * GROUP, 2 * GROUP), :].astype(F32)
        return pair[:GROUP], pair[GROUP:]

    def ends_of(step, piece):
        return [part for k in range(0, 6, 2) for part in two(step, piece, k)]

    def forward(step, _):
        for piece in range(count):
            ends = ends_of(step, piece)
            for k in range(3):
                state = f_ref[piece, at(k), :]
                ahead_ref[step, piece, at(k), :] = state
                f_ref[piece, at(k), :] = factor(step, k) * state + ends[k]
        return 0

    def backward(i, _):
        step = steps - 1 - i
        for piece in range(count):
            ends = ends_of(step, piece)
            states = [ahead_ref[step, piece, at(k), :] for k in range(3)]
            for q in range(3):
                state = f_ref[piece, at(3 + q), :]
                states.append(state)
                total = factor(step, q) * state + ends[3 + q]
                for k in range(3):
                    total += factor(step, 3 + 3 * q + k) * states[k]
                f_ref[piece, at(3 + q), :] = total
            for k in range(0, 6, 2):
                pair = jnp.concatenate([states[k], states[k + 1]], axis=0)
                state_ref[step, piece, pl.ds(k * GROUP, 2 * GROUP), :] = pair.astype(BF16)
        return 0

    lax.fori_loop(0, steps, forward, 0)
    lax.fori_loop(0, steps, backward, 0)


def fill_held(owner, held_ref):
    slabs = owner.shape[1]
    across = jnp.broadcast_to(owner, (slabs, slabs))
    down = across.T
    row, lane = iota((slabs, slabs), 0), iota((slabs, slabs), 1)
    earlier = jnp.where((across == down) & (row < lane), 1.0, 0.0)
    rank = jnp.sum(earlier, axis=0, keepdims=True)
    for slot in range(MOST):
        held_ref[slot] = jnp.where((across == row.astype(F32)) & (rank == slot), 1.0, 0.0)


def whole_rows(left_ref, wide_ref, state_ref, step, sigma, take):
    _, count, lines, lanes = wide_ref.shape
    lanes //= 2
    left = left_ref[block_rows(step), :][:, : lines + 12 * GROUP]
    for piece in range(count):
        states = state_ref[step, piece]
        right = jnp.concatenate([wide_ref[step, piece], states, states], axis=0)
        result = jnp.dot(left, right, preferred_element_type=F32)
        here = pl.ds(piece * 2 * GROUP, 2 * GROUP)
        for r in range(BLOCK):
            part = result[r * GROUP : (r + 1) * GROUP]
            part = jnp.concatenate([part[:, :lanes], part[:, lanes:]], axis=0)
            take(step * BLOCK + r, here, part * sigma)


def final_kernel(
    y_far, wide_far, end_far, local_far, scan_far, owner_ref, sigma_ref, arrived_ref,
    out_ref, peak_ref, wide_ref, arrived, end_ref, y_ref, local_ref, scan_ref, fetched, fetched_small,
    held_ref, f_ref, ahead_ref, state_ref, done_ref, sent, left_ref,
):
    steps = wide_far.shape[0]
    lanes = peak_ref.shape[1]
    pieces = Pieces(wide_far, wide_ref, arrived, TURNS)
    results = Pieces(done_ref, out_ref, sent, TURNS * BLOCK)
    wait_small = start_all([local_far, y_far, scan_far], [local_ref, y_ref, scan_ref], fetched_small)
    wait = start_all([end_far], [end_ref], fetched)
    pieces.start()
    fill_held(owner_ref[...], held_ref)
    wait_small()
    lines = BLOCK * GROUP
    for step in range(steps):
        whole = each_point(local_ref[pl.ds(step * BLOCK, BLOCK), :])
        left_ref[pl.ds(step * lines, lines), :] = whole
    y_carries(y_ref, arrived_ref, f_ref)
    wait()
    scan_blocks(scan_ref, end_ref, f_ref, ahead_ref, state_ref)
    sigma = jnp.broadcast_to(sigma_ref[...], (2 * GROUP, lanes))

    def run(i, most):
        most = list(most)

        def take(row, here, scaled):
            at = len(taken) % 2
            taken.append(row)
            most[at] = jnp.maximum(most[at], jnp.abs(scaled))
            done_ref[row, here, :] = scaled.astype(BF16)

        taken = []
        pieces.copy(i).wait()
        for step in range(TURNS):
            whole_rows(left_ref, wide_ref, state_ref, TURNS * i + step, sigma, take)
        results.copy(i).start()
        return tuple(most)

    start = tuple(jnp.zeros((2 * GROUP, lanes), F32) for _ in range(2))
    most = lax.fori_loop(0, steps // TURNS, run, start)
    peaks = jnp.max(jnp.maximum(*most), axis=0, keepdims=True)
    lane = iota(peak_ref.shape, 1)
    rows = jnp.zeros(peak_ref.shape, F32)
    for slot in range(MOST):
        held = jnp.sum(held_ref[slot] * peaks, axis=1, keepdims=True)
        rows = jnp.where(lane == slot, held, rows)
    peak_ref[...] = rows
    results.wait()


SMEM = pl.BlockSpec(memory_space=pltpu.SMEM)
VMEM = pl.BlockSpec(memory_space=pltpu.VMEM)
HBM = pl.BlockSpec(memory_space=pltpu.HBM)
MIB = 1024 * 1024
FULL = 61
LAST = 55


def call(kernel, name, ins, outs, scratch, mib, us):
    return pl.pallas_call(
        kernel,
        in_specs=ins,
        out_specs=[spec for spec, _ in outs],
        out_shape=[array for _, array in outs],
        scratch_shapes=scratch,
        compiler_params=pltpu.CompilerParams(vmem_limit_bytes=mib * MIB),
        cost_estimate=pl.CostEstimate(flops=0, bytes_accessed=int(us * 3e6), transcendentals=0),
        name=name,
    )


def shape(*dims, kind=BF16):
    return jax.ShapeDtypeStruct(dims, kind)


def copies(count):
    return pltpu.SemaphoreType.DMA((count,))


def x_ends(lat_class, lengths, increments):
    height, width, lanes = increments.shape
    return call(
        ends_kernel,
        "x_ends",
        [SMEM, SMEM, HBM],
        [(VMEM, shape(height * GROUP, lanes))],
        [
            pltpu.VMEM((NCLASS * NCLASS, 2 * GROUP, width), BF16),
            pltpu.VMEM((height, width, lanes), BF16),
            copies(height // LONG),
        ],
        FULL,
        4,
    )(lat_class, lengths, increments)[0]


def tables(lengths, lat_class, count, width, lanes):
    height = lat_class.shape[0] // count
    return call(
        tables_kernel,
        "tables",
        [SMEM, VMEM],
        [
            (VMEM, shape(2 * NCLASS, width, width + 2 * GROUP)),
            (VMEM, shape(width, NCLASS * GROUP)),
            (VMEM, shape(15, count, lanes, kind=F32)),
            (VMEM, shape(GROUP, height * GROUP, kind=F32)),
            (VMEM, shape(6 * GROUP, height * GROUP)),
            (VMEM, shape(6 * GROUP, height * GROUP)),
            (VMEM, shape(height, 2 * lanes)),
            (VMEM, shape(height // BLOCK, 16, lanes, kind=F32)),
        ],
        [],
        FULL,
        6,
    )(lengths, lat_class.reshape(-1, lanes))


def own_y_ends(lat_class, increments, m_table, weights):
    height, width, lanes = increments.shape
    pieces = width // (2 * GROUP)
    block = pltpu.VMEM((pieces, BLOCK * GROUP, 2 * lanes), BF16)
    return call(
        own_ends_kernel,
        "own_y_ends",
        [SMEM, HBM, HBM, HBM],
        [(VMEM, shape(6, width, lanes, kind=F32))],
        [
            pltpu.VMEM((pieces, 6 * GROUP, 2 * lanes), F32),
            block,
            block,
            pltpu.VMEM((height, width, lanes), BF16),
            copies(height // (2 * BLOCK)),
            pltpu.VMEM(m_table.shape, m_table.dtype),
            pltpu.VMEM(weights.shape, weights.dtype),
            copies(2),
        ],
        FULL,
        6,
    )(lat_class, increments, m_table, weights)[0]


def x_scan(lat_class, lengths, ends, width, height):
    _, lines, lanes = ends.shape
    return call(
        functools.partial(scan_kernel, width, height),
        "x_scan",
        [SMEM, SMEM, VMEM],
        [(VMEM, shape(*ends.shape))],
        [pltpu.VMEM((lines, lanes), F32), pltpu.VMEM((lines, lanes), BF16), pltpu.VMEM(ends.shape, F32)],
        8,
        1,
    )(lat_class, lengths, ends)[0]


def y_ends(corner, states, x_table, own, y_table):
    _, width, lanes = own.shape
    return call(
        corner_kernel,
        "y_ends",
        [VMEM] * 5,
        [(VMEM, shape(y_table.shape[1], 3 * width, lanes))],
        [pltpu.VMEM((6, width, lanes), F32)],
        8,
        1,
    )(corner, states, x_table, own, y_table)[0]


def x_filter(lat_class, increments, states, m_table, ends, after):
    height, width, lanes = increments.shape
    pieces = width // (2 * GROUP)
    steps = height // BLOCK
    wide = (steps, pieces, BLOCK * GROUP, 2 * lanes)
    end = (steps, pieces, 6 * GROUP, 2 * lanes)
    return call(
        filter_kernel,
        "x_filter",
        [SMEM] + [HBM] * 5,
        [(HBM, shape(*wide)), (HBM, shape(*end))],
        [pltpu.VMEM(array.shape, array.dtype) for array in (states, m_table, ends)]
        + [
            copies(3),
            pltpu.VMEM(wide[1:], BF16),
            pltpu.VMEM(wide[1:], BF16),
            pltpu.VMEM(wide, BF16),
            pltpu.VMEM(end, BF16),
            pltpu.VMEM((height, width, lanes), BF16),
            copies(steps // 2),
            copies(steps),
            copies(steps),
        ],
        FULL,
        8,
    )(lat_class, increments, states, m_table, ends, after)


def tile_output(y_table, wide, ends, local, scan, owner, sigma, arrived, height, width):
    steps, pieces, lines, lanes = ends.shape
    half = lanes // 2
    return call(
        final_kernel,
        "tile_output",
        [HBM] * 5 + [VMEM] * 3,
        [(HBM, shape(height, width, half)), (VMEM, shape(half, half, kind=F32))],
        [
            pltpu.VMEM(wide.shape, wide.dtype),
            copies(steps // TURNS),
            pltpu.VMEM(ends.shape, ends.dtype),
            pltpu.VMEM(y_table.shape, y_table.dtype),
            pltpu.VMEM(local.shape, local.dtype),
            pltpu.VMEM(scan.shape, scan.dtype),
            copies(1),
            copies(3),
            pltpu.VMEM((MOST, half, half), F32),
            pltpu.VMEM((pieces, lines, lanes), F32),
            pltpu.VMEM((steps, pieces, lines // 2, lanes), F32),
            pltpu.VMEM(ends.shape, BF16),
            pltpu.VMEM((height, width, half), BF16),
            copies(steps // TURNS),
            pltpu.VMEM((height * GROUP, lanes), BF16),
        ],
        LAST,
        8,
    )(y_table, wide, ends, local, scan, owner, sigma, arrived)


def local(increments, lengths, lat_class, slab_owner, level_sigma):
    count_x = lax.axis_size("tx")
    count_y = lax.axis_size("ty")
    height, width, lanes = increments.shape
    lines = height // count_x * GROUP

    ends = x_ends(lat_class, lengths, increments)
    ends, lengths, lat_class = lax.optimization_barrier((ends, lengths, lat_class))
    with jax.named_scope("x_ends_to_scanners"):
        ends = lax.all_to_all(ends.reshape(count_x, lines, lanes), "tx", 0, 0, tiled=True)

    sigma = level_sigma.reshape(1, lanes)
    owner = slab_owner.astype(F32).reshape(1, lanes)
    (
        m_table, x_table, y_table, corner,
        weights, block_ends, block_local, block_scan,
    ) = tables(lengths, lat_class, count_y, width, lanes)

    ends, m_table = lax.optimization_barrier((ends, m_table))
    states = x_scan(lat_class, lengths, ends, width, height)
    with jax.named_scope("x_states_to_tiles"):
        states = lax.all_to_all(states, "tx", 0, 0, tiled=True).reshape(height * GROUP, lanes)
    own = own_y_ends(lat_class, increments, m_table, weights)

    sent = y_ends(corner, states, x_table, own, y_table)
    with jax.named_scope("y_ends_to_column"):
        arrived = lax.all_to_all(sent, "ty", 0, 0, tiled=True)
    wide, ends = x_filter(lat_class, increments, states, m_table, block_ends, sent)

    tile_out, peak_rows = tile_output(
        y_table, wide, ends, block_local, block_scan, owner, sigma, arrived, height, width
    )
    with jax.named_scope("peaks_to_owners"):
        peaks = lax.all_to_all(peak_rows, ("tx", "ty"), 0, 0, tiled=True)
    peak_table = jnp.max(peaks, axis=0, keepdims=True)[:, :MOST]
    return (tile_out, peak_table)


def solution(mesh):
    placed = (P("ty", "tx", None), P(), P(), P(), P())
    return jax.shard_map(
        local,
        mesh=mesh,
        in_specs=placed,
        out_specs=(P("ty", "tx", None), P(("tx", "ty"), None)),
        check_vma=False,
    )
```

profile of v0, /device:TPU:1, one launch (start us, length us, event | category | flops | bytes accessed | tf_op | source)
XLA Modules:
  0.0 81.0 jit_solution(2661879392926968538)
XLA Ops:
  0.6 0.0 copy-start.3
  0.6 0.0 copy-start.6
  0.7 4.3 %x_ends.1 = bf16[1536,128]{1,0:T(8,128)(2,1)} custom-call(s32[1536]{0:T(1024)} %lat_ref.4, f32[4,3]{1,0:T(4,128)} %lengths_ref.3, bf16[192,96,128]{2,1,0:T(8,128)(2,1)} %v_ref.5), custom_call_target="tpu_custom_call" | custom-call | bytes 12000000 | tf_op jit(solution)/shard_map/x_ends/pallas_call | solution.py:704
  5.0 8.6 %all-to-all-start = ((bf16[16,96,128]{2,1,0:T(8,128)(2,1)}), bf16[16,96,128]{2,1,0:T(8,128)(2,1)S(1)}, u32[]{:S(2)}, u32[]{:S(2)}) async-start(bf16[16,96,128]{2,1,0:T(8,128)(2,1)} %bitcast.14), calls=%async_computation | async-start | bytes 786432 | tf_op jit(solution)/shard_map/x_ends_to_scanners/all_to_all | solution.py:858
  13.6 5.7 %tables.1 = (bf16[8,96,112]{2,1,0:T(8,128)(2,1)}, bf16[96,32]{1,0:T(8,128)(2,1)}, f32[15,8,128]{2,1,0:T(8,128)}, f32[8,1536]{1,0:T(8,128)}, bf16[48,1536]{1,0:T(...) custom-call(f32[4,3]{1,0:T(4,128)} %lengths_ref.3, s32[12,128]{1,0:T(8,128)} %bitcast.13), custom_call_target="tpu_custom_call" | custom-call | bytes 18000000 | tf_op jit(solution)/shard_map/tables/pallas_call | solution.py:721
  19.3 0.0 copy-start.2
  19.3 0.0 copy-start.4
  19.3 0.0 copy-start.5
  19.3 2.6 %all-to-all-done.e_ref = bf16[16,96,128]{2,1,0:T(8,128)(2,1)S(1)} async-done(((bf16[16,96,128]{2,1,0:T(8,128)(2,1)}), bf16[16,96,128]{2,1,0:T(8,128)(2,1)S(1)}, u32[]{:S(2)}, u32[]{:S(2)}) %all-to-all-start) | async-done | bytes 393248 | tf_op jit(solution)/shard_map/x_ends_to_scanners/all_to_all | solution.py:858
  21.9 0.0 copy-done.3
  21.9 0.0 copy-done.6
  21.9 0.0 copy-start.8
  21.9 1.9 %x_scan.1 = bf16[16,96,128]{2,1,0:T(8,128)(2,1)} custom-call(s32[1536]{0:T(1024)S(1)} %copy-done.3, f32[4,3]{1,0:T(4,128)S(1)} %copy-done.6, bf16[16,96,128]{2,1,0:T(8,128)(2,1)S(1)} %all-to-all-done.e_ref), custom_call_target="tpu_custom_call" | custom-call | bytes 3000000 | tf_op jit(solution)/shard_map/x_scan/pallas_call | solution.py:767
  23.8 4.1 %all-to-all-start.1 = ((bf16[16,96,128]{2,1,0:T(8,128)(2,1)}), bf16[16,96,128]{2,1,0:T(8,128)(2,1)S(1)}, u32[]{:S(2)}, u32[]{:S(2)}) async-start(bf16[16,96,128]{2,1,0:T(8,128)(2,1)} %x_scan.1), calls=%async_computation.1 | async-start | bytes 786432 | tf_op jit(solution)/shard_map/x_states_to_tiles/all_to_all | solution.py:870
  27.9 6.7 %own_y_ends.1.own_ref = f32[6,96,128]{2,1,0:T(8,128)} custom-call(s32[1536]{0:T(1024)} %lat_ref.4, bf16[192,96,128]{2,1,0:T(8,128)(2,1)} %v_ref.5, bf16[8,96,112]{2,1,0:T(8,128)(2,1)} %get-tuple-element.25.m_far, bf16[48,1536]{1,0:T(8,128)(2,1)} %get-tuple-element.29.weight_far), custom_call_target="tpu_custom_call" | custom-call | bytes 18000000 | tf_op jit(solution)/shard_map/own_y_ends/pallas_call | solution.py:745
  34.6 1.3 %all-to-all-done.1 = bf16[16,96,128]{2,1,0:T(8,128)(2,1)S(1)} async-done(((bf16[16,96,128]{2,1,0:T(8,128)(2,1)}), bf16[16,96,128]{2,1,0:T(8,128)(2,1)S(1)}, u32[]{:S(2)}, u32[]{:S(2)}) %all-to-all-start.1) | async-done | bytes 393248 | tf_op jit(solution)/shard_map/x_states_to_tiles/all_to_all | solution.py:870
  35.9 0.0 copy-start
  35.9 0.0 copy-done.2
  35.9 0.0 copy-done.4
  35.9 0.0 copy-done.5
  35.9 0.0 copy-start.1
  35.9 1.1 %copy-done.1 = f32[6,96,128]{2,1,0:T(8,128)S(1)} copy-done((f32[6,96,128]{2,1,0:T(8,128)S(1)}, f32[6,96,128]{2,1,0:T(8,128)}, u32[]{:S(2)}) %copy-start.1) | copy-done | bytes 294936
  37.0 1.5 %y_ends.1.after_ref = bf16[8,288,128]{2,1,0:T(8,128)(2,1)} custom-call(f32[8,1536]{1,0:T(8,128)S(1)} %copy-done.4, bf16[1536,128]{1,0:T(8,128)(2,1)S(1)} %bitcast.11, bf16[96,32]{1,0:T(8,128)(2,1)S(1)} %copy-done.5, f32[6,96,128]{2,1,0:T(8,128)S(1)} %copy-done.1, f32[15,8,128]{2,1,0:T(8,128)S(1)} %copy-done.2), custom_call_target="tpu_custom_call" | custom-call | bytes 3000000 | tf_op jit(solution)/shard_map/y_ends/pallas_call | solution.py:780
  38.5 7.5 %all-to-all-start.2 = ((bf16[8,288,128]{2,1,0:T(8,128)(2,1)}), bf16[8,288,128]{2,1,0:T(8,128)(2,1)S(1)}, u32[]{:S(2)}, u32[]{:S(2)}) async-start(bf16[8,288,128]{2,1,0:T(8,128)(2,1)} %y_ends.1.after_ref), calls=%async_computation.2 | async-start | bytes 1179648 | tf_op jit(solution)/shard_map/y_ends_to_column/all_to_all | solution.py:875
  46.1 0.0 copy-done.8
  46.1 0.5 convert_bitcast_fusion.owner_ref
  46.6 0.0 copy-done
  46.6 7.2 %x_filter.1 = (bf16[12,6,128,256]{3,2,1,0:T(8,128)(2,1)}, bf16[12,6,48,256]{3,2,1,0:T(8,128)(2,1)}) custom-call(s32[1536]{0:T(1024)} %lat_ref.4, bf16[192,96,128]{2,1,0:T(8,128)(2,1)} %v_ref.5, bf16[1536,128]{1,0:T(8,128)(2,1)} %bitcast.12, bf16[8,96,112]{2,1,0:T(8,128)(2,1)} %get-tuple-element.25.m_far, bf16[48,1536]{1,0:T(8,128)(2,1)} %get-tuple-element.26.ends_far, ...), custom_call_target="tpu_custom_call" | custom-call | bytes 24000000 | tf_op jit(solution)/shard_map/x_filter/pallas_call | solution.py:797
  53.8 2.4 %all-to-all-done.2.arrived_ref = bf16[8,288,128]{2,1,0:T(8,128)(2,1)S(1)} async-done(((bf16[8,288,128]{2,1,0:T(8,128)(2,1)}), bf16[8,288,128]{2,1,0:T(8,128)(2,1)S(1)}, u32[]{:S(2)}, u32[]{:S(2)}) %all-to-all-start.2) | async-done | bytes 589856 | tf_op jit(solution)/shard_map/y_ends_to_column/all_to_all | solution.py:875
  56.3 0.0 copy-start.7
  56.3 0.8 %copy-done.7 = bf16[8,288,128]{2,1,0:T(8,128)(2,1)} copy-done((bf16[8,288,128]{2,1,0:T(8,128)(2,1)}, bf16[8,288,128]{2,1,0:T(8,128)(2,1)S(1)}, u32[]{:S(2)}) %copy-start.7) | copy-done | bytes 589848
  57.1 8.0 %tile_output.1 = (bf16[192,96,128]{2,1,0:T(8,128)(2,1)}, f32[128,128]{1,0:T(8,128)}) custom-call(f32[15,8,128]{2,1,0:T(8,128)} %get-tuple-element.21.y_ref.y_far, bf16[12,6,128,256]{3,2,1,0:T(8,128)(2,1)} %get-tuple-element.30.wide_far, bf16[12,6,48,256]{3,2,1,0:T(8,128)(2,1)} %get-tuple-element.31.end_far, bf16[192,256]{1,0:T(8,128)(2,1)} %get-tuple-element.32.local_far, ...), custom_call_target="tpu_custom_call" | custom-call | bytes 24000000 | tf_op jit(solution)/shard_map/tile_output/pallas_call | solution.py:822
  65.1 15.2 %all_to_all.24 = f32[128,1,128]{2,1,0:T(1,128)S(1)} all-to-all(f32[128,1,128]{2,1,0:T(1,128)} %bitcast.15), channel_id=1, replica_groups=mesh['tx'=16,'ty'=8] {'tx','ty'}, dimensions={0} | all-to-all | bytes 131072 | tf_op jit(solution)/shard_map/peaks_to_owners/all_to_all | solution.py:882
  80.4 0.7 reduce_max.9
Async XLA Ops:
  0.6 21.2 %copy-start.3 = (s32[1536]{0:T(1024)S(1)}, s32[1536]{0:T(1024)}, u32[]{:S(2)}) copy-start(s32[1536]{0:T(1024)} %lat_ref.4) | copy-start | bytes 18436
  0.6 21.2 %copy-start.6 = (f32[4,3]{1,0:T(4,128)S(1)}, f32[4,3]{1,0:T(4,128)}, u32[]{:S(2)}) copy-start(f32[4,3]{1,0:T(4,128)} %lengths_ref.3) | copy-start | bytes 148
  5.0 16.9 %all-to-all-start = ((bf16[16,96,128]{2,1,0:T(8,128)(2,1)}), bf16[16,96,128]{2,1,0:T(8,128)(2,1)S(1)}, u32[]{:S(2)}, u32[]{:S(2)}) async-start(bf16[16,96,128]{2,1,0:T(8,128)(2,1)} %bitcast.14), calls=%async_computation | async-start | bytes 786432 | tf_op jit(solution)/shard_map/x_ends_to_scanners/all_to_all | solution.py:858
  19.3 16.6 %copy-start.2 = (f32[15,8,128]{2,1,0:T(8,128)S(1)}, f32[15,8,128]{2,1,0:T(8,128)}, u32[]{:S(2)}) copy-start(f32[15,8,128]{2,1,0:T(8,128)} %get-tuple-element.21.y_ref.y_far) | copy-start | bytes 184324
  19.3 16.6 %copy-start.4 = (f32[8,1536]{1,0:T(8,128)S(1)}, f32[8,1536]{1,0:T(8,128)}, u32[]{:S(2)}) copy-start(f32[8,1536]{1,0:T(8,128)} %get-tuple-element.27.corner_ref) | copy-start | bytes 147460
  19.3 16.6 %copy-start.5 = (bf16[96,32]{1,0:T(8,128)(2,1)S(1)}, bf16[96,32]{1,0:T(8,128)(2,1)}, u32[]{:S(2)}) copy-start(bf16[96,32]{1,0:T(8,128)(2,1)} %get-tuple-element.28.x_ref) | copy-start | bytes 18436
  21.9 24.2 %copy-start.8 = (s32[128]{0:T(128)S(1)}, s32[128]{0:T(128)}, u32[]{:S(2)}) copy-start(s32[128]{0:T(128)} %param.8) | copy-start | bytes 1540
  23.8 12.1 %all-to-all-start.1 = ((bf16[16,96,128]{2,1,0:T(8,128)(2,1)}), bf16[16,96,128]{2,1,0:T(8,128)(2,1)S(1)}, u32[]{:S(2)}, u32[]{:S(2)}) async-start(bf16[16,96,128]{2,1,0:T(8,128)(2,1)} %x_scan.1), calls=%async_computation.1 | async-start | bytes 786432 | tf_op jit(solution)/shard_map/x_states_to_tiles/all_to_all | solution.py:870
  35.9 10.7 %copy-start = (bf16[16,96,128]{2,1,0:T(8,128)(2,1)}, bf16[16,96,128]{2,1,0:T(8,128)(2,1)S(1)}, u32[]{:S(2)}) copy-start(bf16[16,96,128]{2,1,0:T(8,128)(2,1)S(1)} %all-to-all-done.1) | copy-start | bytes 1179652
  35.9 1.1 %copy-start.1 = (f32[6,96,128]{2,1,0:T(8,128)S(1)}, f32[6,96,128]{2,1,0:T(8,128)}, u32[]{:S(2)}) copy-start(f32[6,96,128]{2,1,0:T(8,128)} %own_y_ends.1.own_ref) | copy-start | bytes 884740
  38.5 17.7 %all-to-all-start.2 = ((bf16[8,288,128]{2,1,0:T(8,128)(2,1)}), bf16[8,288,128]{2,1,0:T(8,128)(2,1)S(1)}, u32[]{:S(2)}, u32[]{:S(2)}) async-start(bf16[8,288,128]{2,1,0:T(8,128)(2,1)} %y_ends.1.after_ref), calls=%async_computation.2 | async-start | bytes 1179648 | tf_op jit(solution)/shard_map/y_ends_to_column/all_to_all | solution.py:875
  56.3 0.8 %copy-start.7 = (bf16[8,288,128]{2,1,0:T(8,128)(2,1)}, bf16[8,288,128]{2,1,0:T(8,128)(2,1)S(1)}, u32[]{:S(2)}) copy-start(bf16[8,288,128]{2,1,0:T(8,128)(2,1)S(1)} %all-to-all-done.2.arrived_ref) | copy-start | bytes 1769476
where the time goes:
time: 81.7 us; the launch traced here: 81 us
  Pallas kernels  35.4 us (43%)
  starting transfers between devices  20.3 us (25%)
  blocking collectives  15.2 us (19%)
  waiting for transfers between devices  6.3 us (8%)
  local copies, waits for them, and re-layouts  1.97 us (2%)
  other arithmetic  1.17 us (1%)
    all_to_all x1, blocking collectives, local(): peaks = lax.all_to_all(peak_rows, ('tx', 'ty'), 0, 0, tiled=True)  15.2 us
    all_to_all x1, starting transfers between devices, local(): lax.all_to_all(ends.reshape(count_x, lines, lanes), 'tx', 0, 0, tiled=True)  8.61 us
    pallas_call x1, Pallas kernels, tile_output(): call(final_kernel, 'tile_output', [HBM] * 5 + [VMEM] * 3, [(HBM, shape(he...  8.04 us
    all_to_all x1, starting transfers between devices, local(): arrived = lax.all_to_all(sent, 'ty', 0, 0, tiled=True)  7.55 us
    pallas_call x1, Pallas kernels, x_filter(): call(filter_kernel, 'x_filter', [SMEM] + [HBM] * 5, [(HBM, shape(*wide)),...  7.24 us
    pallas_call x1, Pallas kernels, own_y_ends(): call(own_ends_kernel, 'own_y_ends', [SMEM, HBM, HBM, HBM], [(VMEM, shape(...  6.65 us
    pallas_call x1, Pallas kernels, tables(): call(tables_kernel, 'tables', [SMEM, VMEM], [(VMEM, shape(2 * NCLASS, wid...  5.68 us
    pallas_call x1, Pallas kernels, x_ends(): call(ends_kernel, 'x_ends', [SMEM, SMEM, HBM], [(VMEM, shape(height * GRO...  4.32 us
  transfers between devices with their start and end apart: 3, of which 3 were waited for; matrix products, arithmetic and copies ran while one was open for 1% of the time, Pallas kernels for 24%

commit v1 on v0

--- a/solution.py
+++ b/solution.py
@@ -627,7 +627,7 @@
     steps = wide_far.shape[0]
     lanes = peak_ref.shape[1]
     pieces = Pieces(wide_far, wide_ref, arrived, TURNS)
-    results = Pieces(done_ref, out_ref, sent, TURNS * BLOCK)
+    results = Pieces(done_ref, out_ref, sent, TURNS // 2 * BLOCK)
     wait_small = start_all([local_far, y_far, scan_far], [local_ref, y_ref, scan_ref], fetched_small)
     wait = start_all([end_far], [end_ref], fetched)
     pieces.start()
@@ -655,7 +655,8 @@
         pieces.copy(i).wait()
         for step in range(TURNS):
             whole_rows(left_ref, wide_ref, state_ref, TURNS * i + step, sigma, take)
-        results.copy(i).start()
+            if step % (TURNS // 2) == TURNS // 2 - 1:
+                results.copy(2 * i + step // (TURNS // 2)).start()
         return tuple(most)
 
     start = tuple(jnp.zeros((2 * GROUP, lanes), F32) for _ in range(2))
@@ -838,7 +839,7 @@
             pltpu.VMEM((steps, pieces, lines // 2, lanes), F32),
             pltpu.VMEM(ends.shape, BF16),
             pltpu.VMEM((height, width, half), BF16),
-            copies(steps // TURNS),
+            copies(2 * steps // TURNS),
             pltpu.VMEM((height * GROUP, lanes), BF16),
         ],
         LAST,

time: 81.7 us -> 81.4 us (level)
  no operation moved by 1% of the time
where the time goes in v1:
time: 81.4 us; the launch traced here: 80.8 us
  Pallas kernels  35.1 us (43%)
  starting transfers between devices  20.3 us (25%)
  blocking collectives  15.2 us (19%)
  waiting for transfers between devices  6.28 us (8%)
  local copies, waits for them, and re-layouts  1.97 us (2%)
  other arithmetic  1.17 us (1%)
    all_to_all x1, blocking collectives, local(): peaks = lax.all_to_all(peak_rows, ('tx', 'ty'), 0, 0, tiled=True)  15.2 us
    all_to_all x1, starting transfers between devices, local(): lax.all_to_all(ends.reshape(count_x, lines, lanes), 'tx', 0, 0, tiled=True)  8.61 us
    pallas_call x1, Pallas kernels, tile_output(): call(final_kernel, 'tile_output', [HBM] * 5 + [VMEM] * 3, [(HBM, shape(he...  7.74 us
    all_to_all x1, starting transfers between devices, local(): arrived = lax.all_to_all(sent, 'ty', 0, 0, tiled=True)  7.55 us
    pallas_call x1, Pallas kernels, x_filter(): call(filter_kernel, 'x_filter', [SMEM] + [HBM] * 5, [(HBM, shape(*wide)),...  7.24 us
    pallas_call x1, Pallas kernels, own_y_ends(): call(own_ends_kernel, 'own_y_ends', [SMEM, HBM, HBM, HBM], [(VMEM, shape(...  6.67 us
    pallas_call x1, Pallas kernels, tables(): call(tables_kernel, 'tables', [SMEM, VMEM], [(VMEM, shape(2 * NCLASS, wid...  5.68 us
    pallas_call x1, Pallas kernels, x_ends(): call(ends_kernel, 'x_ends', [SMEM, SMEM, HBM], [(VMEM, shape(height * GRO...  4.32 us
  transfers between devices with their start and end apart: 3, of which 3 were waited for; matrix products, arithmetic and copies ran while one was open for 1% of the time, Pallas kernels for 24%

profile of v1, /device:TPU:1, one launch (start us, length us, event | category | flops | bytes accessed | tf_op | source)
XLA Modules:
  0.0 80.8 jit_solution(13810983320763468106)
XLA Ops:
  0.6 0.0 copy-start.3
  0.6 0.0 copy-start.6
  0.7 4.3 %x_ends.1 = bf16[1536,128]{1,0:T(8,128)(2,1)} custom-call(s32[1536]{0:T(1024)} %lat_ref.4, f32[4,3]{1,0:T(4,128)} %lengths_ref.3, bf16[192,96,128]{2,1,0:T(8,128)(2,1)} %v_ref.5), custom_call_target="tpu_custom_call" | custom-call | bytes 12000000 | tf_op jit(solution)/shard_map/x_ends/pallas_call | solution.py:705
  5.0 8.6 %all-to-all-start = ((bf16[16,96,128]{2,1,0:T(8,128)(2,1)}), bf16[16,96,128]{2,1,0:T(8,128)(2,1)S(1)}, u32[]{:S(2)}, u32[]{:S(2)}) async-start(bf16[16,96,128]{2,1,0:T(8,128)(2,1)} %bitcast.14), calls=%async_computation | async-start | bytes 786432 | tf_op jit(solution)/shard_map/x_ends_to_scanners/all_to_all | solution.py:859
  13.6 5.7 %tables.1 = (bf16[8,96,112]{2,1,0:T(8,128)(2,1)}, bf16[96,32]{1,0:T(8,128)(2,1)}, f32[15,8,128]{2,1,0:T(8,128)}, f32[8,1536]{1,0:T(8,128)}, bf16[48,1536]{1,0:T(...) custom-call(f32[4,3]{1,0:T(4,128)} %lengths_ref.3, s32[12,128]{1,0:T(8,128)} %bitcast.13), custom_call_target="tpu_custom_call" | custom-call | bytes 18000000 | tf_op jit(solution)/shard_map/tables/pallas_call | solution.py:722
  19.3 0.0 copy-start.2
  19.3 0.0 copy-start.4
  19.3 0.0 copy-start.5
  19.3 2.6 %all-to-all-done.e_ref = bf16[16,96,128]{2,1,0:T(8,128)(2,1)S(1)} async-done(((bf16[16,96,128]{2,1,0:T(8,128)(2,1)}), bf16[16,96,128]{2,1,0:T(8,128)(2,1)S(1)}, u32[]{:S(2)}, u32[]{:S(2)}) %all-to-all-start) | async-done | bytes 393248 | tf_op jit(solution)/shard_map/x_ends_to_scanners/all_to_all | solution.py:859
  21.9 0.0 copy-done.3
  21.9 0.0 copy-done.6
  21.9 0.0 copy-start.8
  21.9 1.9 %x_scan.1 = bf16[16,96,128]{2,1,0:T(8,128)(2,1)} custom-call(s32[1536]{0:T(1024)S(1)} %copy-done.3, f32[4,3]{1,0:T(4,128)S(1)} %copy-done.6, bf16[16,96,128]{2,1,0:T(8,128)(2,1)S(1)} %all-to-all-done.e_ref), custom_call_target="tpu_custom_call" | custom-call | bytes 3000000 | tf_op jit(solution)/shard_map/x_scan/pallas_call | solution.py:768
  23.8 4.1 %all-to-all-start.1 = ((bf16[16,96,128]{2,1,0:T(8,128)(2,1)}), bf16[16,96,128]{2,1,0:T(8,128)(2,1)S(1)}, u32[]{:S(2)}, u32[]{:S(2)}) async-start(bf16[16,96,128]{2,1,0:T(8,128)(2,1)} %x_scan.1), calls=%async_computation.1 | async-start | bytes 786432 | tf_op jit(solution)/shard_map/x_states_to_tiles/all_to_all | solution.py:871
  27.9 6.7 %own_y_ends.1.own_ref = f32[6,96,128]{2,1,0:T(8,128)} custom-call(s32[1536]{0:T(1024)} %lat_ref.4, bf16[192,96,128]{2,1,0:T(8,128)(2,1)} %v_ref.5, bf16[8,96,112]{2,1,0:T(8,128)(2,1)} %get-tuple-element.25.m_far, bf16[48,1536]{1,0:T(8,128)(2,1)} %get-tuple-element.29.weight_far), custom_call_target="tpu_custom_call" | custom-call | bytes 18000000 | tf_op jit(solution)/shard_map/own_y_ends/pallas_call | solution.py:746
  34.6 1.3 %all-to-all-done.1 = bf16[16,96,128]{2,1,0:T(8,128)(2,1)S(1)} async-done(((bf16[16,96,128]{2,1,0:T(8,128)(2,1)}), bf16[16,96,128]{2,1,0:T(8,128)(2,1)S(1)}, u32[]{:S(2)}, u32[]{:S(2)}) %all-to-all-start.1) | async-done | bytes 393248 | tf_op jit(solution)/shard_map/x_states_to_tiles/all_to_all | solution.py:871
  35.9 0.0 copy-start
  35.9 0.0 copy-done.2
  35.9 0.0 copy-done.4
  35.9 0.0 copy-done.5
  35.9 0.0 copy-start.1
  35.9 1.1 %copy-done.1 = f32[6,96,128]{2,1,0:T(8,128)S(1)} copy-done((f32[6,96,128]{2,1,0:T(8,128)S(1)}, f32[6,96,128]{2,1,0:T(8,128)}, u32[]{:S(2)}) %copy-start.1) | copy-done | bytes 294936
  37.0 1.5 %y_ends.1.after_ref = bf16[8,288,128]{2,1,0:T(8,128)(2,1)} custom-call(f32[8,1536]{1,0:T(8,128)S(1)} %copy-done.4, bf16[1536,128]{1,0:T(8,128)(2,1)S(1)} %bitcast.11, bf16[96,32]{1,0:T(8,128)(2,1)S(1)} %copy-done.5, f32[6,96,128]{2,1,0:T(8,128)S(1)} %copy-done.1, f32[15,8,128]{2,1,0:T(8,128)S(1)} %copy-done.2), custom_call_target="tpu_custom_call" | custom-call | bytes 3000000 | tf_op jit(solution)/shard_map/y_ends/pallas_call | solution.py:781
  38.5 7.5 %all-to-all-start.2 = ((bf16[8,288,128]{2,1,0:T(8,128)(2,1)}), bf16[8,288,128]{2,1,0:T(8,128)(2,1)S(1)}, u32[]{:S(2)}, u32[]{:S(2)}) async-start(bf16[8,288,128]{2,1,0:T(8,128)(2,1)} %y_ends.1.after_ref), calls=%async_computation.2 | async-start | bytes 1179648 | tf_op jit(solution)/shard_map/y_ends_to_column/all_to_all | solution.py:876
  46.1 0.0 copy-done.8
  46.1 0.5 convert_bitcast_fusion.owner_ref
  46.6 0.0 copy-done
  46.6 7.2 %x_filter.1 = (bf16[12,6,128,256]{3,2,1,0:T(8,128)(2,1)}, bf16[12,6,48,256]{3,2,1,0:T(8,128)(2,1)}) custom-call(s32[1536]{0:T(1024)} %lat_ref.4, bf16[192,96,128]{2,1,0:T(8,128)(2,1)} %v_ref.5, bf16[1536,128]{1,0:T(8,128)(2,1)} %bitcast.12, bf16[8,96,112]{2,1,0:T(8,128)(2,1)} %get-tuple-element.25.m_far, bf16[48,1536]{1,0:T(8,128)(2,1)} %get-tuple-element.26.ends_far, ...), custom_call_target="tpu_custom_call" | custom-call | bytes 24000000 | tf_op jit(solution)/shard_map/x_filter/pallas_call | solution.py:798
  53.8 2.4 %all-to-all-done.2.arrived_ref = bf16[8,288,128]{2,1,0:T(8,128)(2,1)S(1)} async-done(((bf16[8,288,128]{2,1,0:T(8,128)(2,1)}), bf16[8,288,128]{2,1,0:T(8,128)(2,1)S(1)}, u32[]{:S(2)}, u32[]{:S(2)}) %all-to-all-start.2) | async-done | bytes 589856 | tf_op jit(solution)/shard_map/y_ends_to_column/all_to_all | solution.py:876
  56.3 0.0 copy-start.7
  56.3 0.8 %copy-done.7 = bf16[8,288,128]{2,1,0:T(8,128)(2,1)} copy-done((bf16[8,288,128]{2,1,0:T(8,128)(2,1)}, bf16[8,288,128]{2,1,0:T(8,128)(2,1)S(1)}, u32[]{:S(2)}) %copy-start.7) | copy-done | bytes 589848
  57.1 7.7 %tile_output.1 = (bf16[192,96,128]{2,1,0:T(8,128)(2,1)}, f32[128,128]{1,0:T(8,128)}) custom-call(f32[15,8,128]{2,1,0:T(8,128)} %get-tuple-element.21.y_ref.y_far, bf16[12,6,128,256]{3,2,1,0:T(8,128)(2,1)} %get-tuple-element.30.wide_far, bf16[12,6,48,256]{3,2,1,0:T(8,128)(2,1)} %get-tuple-element.31.end_far, bf16[192,256]{1,0:T(8,128)(2,1)} %get-tuple-element.32.local_far, ...), custom_call_target="tpu_custom_call" | custom-call | bytes 24000000 | tf_op jit(solution)/shard_map/tile_output/pallas_call | solution.py:823
  64.8 15.2 %all_to_all.24 = f32[128,1,128]{2,1,0:T(1,128)S(1)} all-to-all(f32[128,1,128]{2,1,0:T(1,128)} %bitcast.15), channel_id=1, replica_groups=mesh['tx'=16,'ty'=8] {'tx','ty'}, dimensions={0} | all-to-all | bytes 131072 | tf_op jit(solution)/shard_map/peaks_to_owners/all_to_all | solution.py:883
  80.1 0.7 reduce_max.9
Async XLA Ops:
  0.6 21.2 %copy-start.3 = (s32[1536]{0:T(1024)S(1)}, s32[1536]{0:T(1024)}, u32[]{:S(2)}) copy-start(s32[1536]{0:T(1024)} %lat_ref.4) | copy-start | bytes 18436
  0.6 21.2 %copy-start.6 = (f32[4,3]{1,0:T(4,128)S(1)}, f32[4,3]{1,0:T(4,128)}, u32[]{:S(2)}) copy-start(f32[4,3]{1,0:T(4,128)} %lengths_ref.3) | copy-start | bytes 148
  5.0 16.9 %all-to-all-start = ((bf16[16,96,128]{2,1,0:T(8,128)(2,1)}), bf16[16,96,128]{2,1,0:T(8,128)(2,1)S(1)}, u32[]{:S(2)}, u32[]{:S(2)}) async-start(bf16[16,96,128]{2,1,0:T(8,128)(2,1)} %bitcast.14), calls=%async_computation | async-start | bytes 786432 | tf_op jit(solution)/shard_map/x_ends_to_scanners/all_to_all | solution.py:859
  19.3 16.6 %copy-start.2 = (f32[15,8,128]{2,1,0:T(8,128)S(1)}, f32[15,8,128]{2,1,0:T(8,128)}, u32[]{:S(2)}) copy-start(f32[15,8,128]{2,1,0:T(8,128)} %get-tuple-element.21.y_ref.y_far) | copy-start | bytes 184324
  19.3 16.6 %copy-start.4 = (f32[8,1536]{1,0:T(8,128)S(1)}, f32[8,1536]{1,0:T(8,128)}, u32[]{:S(2)}) copy-start(f32[8,1536]{1,0:T(8,128)} %get-tuple-element.27.corner_ref) | copy-start | bytes 147460
  19.3 16.6 %copy-start.5 = (bf16[96,32]{1,0:T(8,128)(2,1)S(1)}, bf16[96,32]{1,0:T(8,128)(2,1)}, u32[]{:S(2)}) copy-start(bf16[96,32]{1,0:T(8,128)(2,1)} %get-tuple-element.28.x_ref) | copy-start | bytes 18436
  21.9 24.2 %copy-start.8 = (s32[128]{0:T(128)S(1)}, s32[128]{0:T(128)}, u32[]{:S(2)}) copy-start(s32[128]{0:T(128)} %param.8) | copy-start | bytes 1540
  23.8 12.1 %all-to-all-start.1 = ((bf16[16,96,128]{2,1,0:T(8,128)(2,1)}), bf16[16,96,128]{2,1,0:T(8,128)(2,1)S(1)}, u32[]{:S(2)}, u32[]{:S(2)}) async-start(bf16[16,96,128]{2,1,0:T(8,128)(2,1)} %x_scan.1), calls=%async_computation.1 | async-start | bytes 786432 | tf_op jit(solution)/shard_map/x_states_to_tiles/all_to_all | solution.py:871
  35.9 10.7 %copy-start = (bf16[16,96,128]{2,1,0:T(8,128)(2,1)}, bf16[16,96,128]{2,1,0:T(8,128)(2,1)S(1)}, u32[]{:S(2)}) copy-start(bf16[16,96,128]{2,1,0:T(8,128)(2,1)S(1)} %all-to-all-done.1) | copy-start | bytes 1179652
  35.9 1.1 %copy-start.1 = (f32[6,96,128]{2,1,0:T(8,128)S(1)}, f32[6,96,128]{2,1,0:T(8,128)}, u32[]{:S(2)}) copy-start(f32[6,96,128]{2,1,0:T(8,128)} %own_y_ends.1.own_ref) | copy-start | bytes 884740
  38.5 17.7 %all-to-all-start.2 = ((bf16[8,288,128]{2,1,0:T(8,128)(2,1)}), bf16[8,288,128]{2,1,0:T(8,128)(2,1)S(1)}, u32[]{:S(2)}, u32[]{:S(2)}) async-start(bf16[8,288,128]{2,1,0:T(8,128)(2,1)} %y_ends.1.after_ref), calls=%async_computation.2 | async-start | bytes 1179648 | tf_op jit(solution)/shard_map/y_ends_to_column/all_to_all | solution.py:876
  56.3 0.8 %copy-start.7 = (bf16[8,288,128]{2,1,0:T(8,128)(2,1)}, bf16[8,288,128]{2,1,0:T(8,128)(2,1)S(1)}, u32[]{:S(2)}) copy-start(bf16[8,288,128]{2,1,0:T(8,128)(2,1)S(1)} %all-to-all-done.2.arrived_ref) | copy-start | bytes 1769476
